TPU v7x, 32 devices: a whole 2x2x4 slice. The times are simulated.
32 devices in a mesh: dp: 2 (over y), expert: 4 (over x, core), hid: 4 (over z).
Axes of the slice: x: 2, y: 2, z: 4, core: 2. Of those that a mesh axis runs over, the one named last changes fastest.
Arguments:
- images_in: bfloat16 [32, 256, 1024], P(('dp', 'expert', 'hid')), may hold values from -16 to 16
- slot_keys: bfloat16 [1024, 16], replicated, may hold values from -6 to 6
- w_in: bfloat16 [8, 1024, 4096], P('expert', None, 'hid'), may hold values from -0.1875 to 0.1875
- w_out: bfloat16 [8, 4096, 1024], P('expert', 'hid'), may hold values from -0.09375 to 0.09375
Outputs:
- mixed: bfloat16 [32, 256, 1024], P(('dp', 'expert', 'hid'))
All inputs are finite; a program needn't handle non-finite values.
Results may differ from a plain program's by a relative error of at most 0.013.
Values may be sent and summed in bfloat16 or wider, within the bound.
A program may use at most 64 MiB of HBM per device.

v0:
```python
import jax
import jax.numpy as jnp
from jax import lax
from jax.sharding import PartitionSpec as P

SLOTS = 2


def normal_rows(values):
    floats = values.astype(jnp.float32)
    return (floats * lax.rsqrt(jnp.mean(floats * floats, axis=-1, keepdims=True) + 1e-06)).astype(
        jnp.bfloat16
    )


def unit_columns(values):
    floats = values.astype(jnp.float32)
    return (floats * lax.rsqrt(jnp.sum(floats * floats, axis=0, keepdims=True) + 1e-06)).astype(
        jnp.bfloat16
    )


def body(images_in, slot_keys, w_in, w_out):
    unit_keys = unit_columns(slot_keys)
    normed = normal_rows(images_in)
    logits = 2.0 * jnp.einsum("itd,de->ite", normed, unit_keys, preferred_element_type=jnp.float32)
    powers = jnp.exp(logits)
    dispatch = (powers / jnp.sum(powers, axis=1, keepdims=True)).astype(jnp.bfloat16)
    combine = (powers / jnp.sum(powers, axis=2, keepdims=True)).astype(jnp.bfloat16)
    slot_in = jnp.einsum(
        "ite,itd->ied", dispatch, images_in, preferred_element_type=jnp.float32
    ).astype(jnp.bfloat16)
    owners = lax.axis_size("expert")
    shares = lax.axis_size("hid")
    local_experts = w_in.shape[0]
    d_width = w_in.shape[1]
    images = images_in.shape[0]
    grouped = slot_in.reshape(images, owners, local_experts * SLOTS, d_width)
    arrived = lax.all_to_all(grouped, "expert", split_axis=1, concat_axis=1, tiled=True)
    arrived = lax.all_gather(arrived, "hid", axis=0, tiled=True)
    slot_rows = arrived.reshape(shares * images * owners, local_experts, SLOTS, d_width)
    hidden = jax.nn.gelu(
        jnp.einsum("rbsd,bdf->rbsf", slot_rows, w_in, preferred_element_type=jnp.float32),
        approximate=True,
    ).astype(jnp.bfloat16)
    partial_value = jnp.einsum("rbsf,bfd->rbsd", hidden, w_out, preferred_element_type=jnp.float32)
    partial_value = partial_value.reshape(shares * images, owners, local_experts * SLOTS, d_width)
    summed = lax.psum_scatter(
        partial_value.astype(jnp.bfloat16), "hid", scatter_dimension=0, tiled=True
    )
    results = lax.all_to_all(summed, "expert", split_axis=1, concat_axis=1, tiled=True)
    results = results.reshape(images, owners * local_experts * SLOTS, d_width)
    return jnp.einsum("ite,ied->itd", combine, results, preferred_element_type=jnp.float32).astype(
        jnp.bfloat16
    )


def solution(mesh):
    return jax.shard_map(
        body,
        mesh=mesh,
        in_specs=(
            P(("dp", "expert", "hid"), None, None),
            P(),
            P("expert", None, "hid"),
            P("expert", "hid", None),
        ),
        out_specs=P(("dp", "expert", "hid"), None, None),
        check_vma=False,
    )
```

profile of v0, /device:TPU:0, one launch (start us, length us, event | category | flops | bytes accessed | tf_op | source)
XLA Modules:
  0.0 89.7 jit_solution(2989323705086775596)
XLA Ops:
  6.5 0.0 all-reduce.3.cloned.1.call-start
  6.5 0.9 fusion.34
  7.4 1.2 %fusion.15 = f32[256]{0:T(256)S(1)} fusion(bf16[1,256,1024]{2,1,0:T(8,128)(2,1)} %param.4), kind=kLoop, calls=%fused_computation.14 | loop fusion | flops 786176 | bytes 525312 | tf_op jit(solution)/shard_map/reduce_sum | solution.py:11
  8.7 1.5 %fusion.48 = (f32[256]{0:T(256)S(1)}, f32[16]{0:T(128)S(1)}, f32[256,16]{0,1:T(8,128)S(1)}) fusion(bf16[1024,16]{0,1:T(8,128)(2,1)} %param.5, f32[16]{0:T(128)S(1)} %add_rsqrt_fusion.1, bf16[1,256,1024]{2,1,0:T(8,128)(2,1)} %param.4, f32[256]{0:T(256)S(1)} %add_rsqrt_fusion), kind=kOutput, calls=%fused_computation.45 | convolution fusion | flops 9236208 | bytes 575616 | tf_op jit(solution)/shard_map/itd,de->ite/dot_general | solution.py:26
  10.2 1.3 %convolution_convert_fusion.1 = bf16[16,1024]{1,0:T(8,128)(2,1)S(1)} fusion(bf16[1,256,1024]{2,1,0:T(8,128)(2,1)} %param.4, f32[256,16]{0,1:T(8,128)S(1)} %get-tuple-element.7, f32[16]{0:T(128)S(1)} %get-tuple-element.6), kind=kOutput, calls=%fused_computation.11 | convolution fusion | flops 8413184 | bytes 573504 | tf_op jit(solution)/shard_map/ite,itd->ied/dot_general | solution.py:30
  11.5 8.0 %all_to_all.10 = bf16[1,4,4,1024]{3,2,0,1:T(4,128)(2,1)S(1)} all-to-all(bf16[1,4,4,1024]{3,2,0,1:T(4,128)(2,1)S(1)} %bitcast.55), channel_id=1, replica_groups=mesh['dp'=2,'expert'=4,'hid'=4] {'expert'}, dimensions={1} | all-to-all | bytes 65536 | tf_op jit(solution)/shard_map/all_to_all | solution.py:39
  19.4 13.7 %all_gather.3 = bf16[4,4,4,1024]{3,2,1,0:T(4,128)(2,1)S(1)} all-gather(bf16[1,4,4,1024]{3,2,1,0:T(4,128)(2,1)S(1)} %bitcast.54), channel_id=1, replica_groups=mesh['dp'=2,'expert'=4,'hid'=4] {'hid'}, dimensions={0}, use_global_device_ids=true | all-gather | bytes 163840 | tf_op jit(solution)/shard_map/all_gather | solution.py:40
  33.1 0.1 reshape.71
  33.2 0.0 copy-start
  33.2 5.0 %fusion.11 = bf16[16,2,2,1024]{3,0,2,1:T(8,128)(2,1)S(1)} fusion(bf16[2,1024,1024]{2,1,0:T(8,128)(2,1)} %param.7, bf16[2,1024,1024]{2,1,0:T(8,128)(2,1)} %param.6, bf16[16,2,2,1024]{3,2,1,0:T(2,128)(2,1)S(1)} %reshape.71), kind=kOutput, calls=%fused_computation.10 | convolution fusion | flops 269090816 | bytes 8650752 | tf_op jit(solution)/shard_map/rbsf,bfd->rbsd/dot_general | solution.py:46
  38.2 0.1 convert_element_type.52
  38.3 0.8 copy.11
  39.0 0.0 all-reduce.3.cloned.1.call-update
  39.1 0.0 copy-done
  39.1 0.6 dynamic-slice
  39.7 34.3 %all-reduce.3.cloned.1.call-done = bf16[4,4,4,1024]{3,2,1,0:T(4,128)(2,1)} async-done(((bf16[4,4,4,1024]{3,2,1,0:T(4,128)(2,1)}), bf16[4,4,4,1024]{3,2,1,0:T(4,128)(2,1)}) %all-reduce.3.cloned.1.call-update) | async-done | bytes 131088
  74.0 1.3 %dynamic-slice_bitcast_fusion = bf16[1,4,4,1024]{3,2,0,1:T(4,128)(2,1)S(1)} fusion(bf16[4,4,4,1024]{3,2,1,0:T(4,128)(2,1)} %all-reduce.3.cloned.1.call-done, u32[]{:T(128)} %bitcast.14), kind=kLoop, calls=%fused_computation.33 | loop fusion | bytes 65540 | tf_op jit(solution)/shard_map/reduce_scatter | solution.py:48
  75.3 6.4 %all_to_all.11 = bf16[1,4,4,1024]{3,2,0,1:T(4,128)(2,1)S(1)} all-to-all(bf16[1,4,4,1024]{3,2,0,1:T(4,128)(2,1)S(1)} %dynamic-slice_bitcast_fusion), channel_id=1, replica_groups=mesh['dp'=2,'expert'=4,'hid'=4] {'expert'}, dimensions={1} | all-to-all | bytes 65536 | tf_op jit(solution)/shard_map/all_to_all | solution.py:51
  81.8 1.1 %fusion.4 = bf16[1,256,1024]{2,1,0:T(8,128)(2,1)} fusion(bf16[16,1024]{1,0:T(8,128)(2,1)S(1)} %reshape.68, f32[256,16]{0,1:T(8,128)S(1)} %get-tuple-element.7, f32[256]{0:T(256)S(1)} %get-tuple-element.5), kind=kOutput, calls=%fused_computation.7 | convolution fusion | flops 8658944 | bytes 574464 | tf_op jit(solution)/shard_map/ite,ied->itd/dot_general | solution.py:53
  (4 shorter events, 0.1 us)
Async XLA Ops:
  6.5 67.4 %all-reduce.3.cloned.1.call-start = ((), (), s32[]{:S(2)}) async-start(), calls=%async_computation.2 | async-start | bytes 262144
  33.2 5.9 %copy-start = (u32[32]{0:T(128)S(1)}, u32[32]{0:T(128)}, u32[]{:S(2)}) copy-start(u32[32]{0:T(128)} %constant.23) | copy-start | bytes 388
Sparse Core Ops, SparseCore 0:
  39.2 34.7 all-reduce.2
where the time goes:
time: 90.2 us; the launch traced here: 89.7 us
  waiting for transfers between devices  34.3 us (38%)
  blocking collectives  28.1 us (31%)
  between operations  13.4 us (15%)
  matrix products  8.95 us (10%)
  local copies, waits for them, and re-layouts  2.83 us (3%)
  other arithmetic  2.12 us (2%)
    unnamed x2, waiting for transfers between devices  34.3 us
    all_gather x1, blocking collectives, body(): arrived = lax.all_gather(arrived, 'hid', axis=0, tiled=True)  13.7 us
    all_to_all x1, blocking collectives, body(): lax.all_to_all(grouped, 'expert', split_axis=1, concat_axis=1, tiled=True)  7.95 us
    all_to_all x1, blocking collectives, body(): lax.all_to_all(summed, 'expert', split_axis=1, concat_axis=1, tiled=True)  6.43 us
    dot_general x1, matrix products, body(): jnp.einsum('rbsf,bfd->rbsd', hidden, w_out, preferred_element_type=jnp.fl...  5.04 us
  transfers between devices with their start and end apart: 1, of which 1 were waited for; matrix products, arithmetic and copies ran while one was open for 1% of the time, Pallas kernels for 0%

commit v1 on v0

v1 whole, which is shorter than its diff:
```python
import functools

import jax
import jax.numpy as jnp
from jax import lax
from jax.experimental import pallas as pl
from jax.experimental.pallas import tpu as pltpu
from jax.sharding import PartitionSpec as P

SLOTS = 2
LANES = 128
ROWS = 16
MESH = pl.DeviceIdType.MESH


def each(count, step):
    if count <= 16:
        for s in range(1, count):
            step(s)
    else:

        def one(s, carry):
            step(s)
            return carry

        lax.fori_loop(1, count, one, 0)


def one_hot(hit):
    return jnp.where(hit, 1.0, 0.0).astype(jnp.bfloat16)


def dot(a, b, dims=((1,), (0,))):
    return lax.dot_general(a, b, (dims, ((), ())), preferred_element_type=jnp.float32)


def kernel(
    owners,
    shares,
    x_hbm,
    keys_hbm,
    w_in_hbm,
    w_out_hbm,
    out,
    x_v,
    keys_v,
    w_in_v,
    w_out_v,
    send_in,
    recv_in,
    send_out,
    recv_out,
    spread_v,
    local_sem,
    send_sem,
    recv_sem,
):
    peers = owners * shares
    tokens, width = x_v.shape
    experts, _, units = w_in_v.shape
    own = experts * SLOTS
    columns = keys_v.shape[0]
    fold = ROWS // own
    part = width // fold
    me_e = lax.axis_index("expert")
    me_h = lax.axis_index("hid")
    me = me_e * shares + me_h

    x_copy = pltpu.make_async_copy(x_hbm.at[0], x_v, local_sem.at[0])
    keys_copy = pltpu.make_async_copy(keys_hbm, keys_v, local_sem.at[1])
    x_copy.start()
    keys_copy.start()

    def peer(s):
        p = lax.rem(me + s, peers)
        e = lax.div(p, shares)
        return p, e, {"expert": e, "hid": lax.rem(p, shares)}

    barrier = pltpu.get_barrier_semaphore()

    def greet(s):
        pl.semaphore_signal(barrier, inc=1, device_id=peer(s)[2], device_id_type=MESH)

    each(peers, greet)

    keys_copy.wait()
    keys = keys_v[...].astype(jnp.float32)
    unit = (keys * lax.rsqrt(jnp.sum(keys * keys, axis=1, keepdims=True) + 1e-06)).astype(
        jnp.bfloat16
    )
    x_copy.wait()
    weights = []
    for e in range(experts):
        for k, (hbm, vmem) in enumerate(((w_in_hbm, w_in_v), (w_out_hbm, w_out_v))):
            weights.append(
                pltpu.make_async_copy(hbm.at[e], vmem.at[e], local_sem.at[2 + 2 * e + k])
            )
    for copy in weights[0::2] + weights[1::2]:
        copy.start()

    x = x_v[...]
    logits = dot(unit, x, ((1,), (1,)))
    squares = None
    for start in range(0, width, LANES):
        floats = x[:, start : start + LANES].astype(jnp.float32)
        squares = floats * floats if squares is None else squares + floats * floats
    high = squares.astype(jnp.bfloat16)
    low = (squares - high.astype(jnp.float32)).astype(jnp.bfloat16)
    ones = jnp.ones((ROWS, LANES), jnp.bfloat16)
    total = dot(ones, high, ((1,), (1,))) + dot(ones, low, ((1,), (1,)))
    scale = 2.0 * lax.rsqrt(total[0:1] * (1.0 / width) + 1e-06)
    powers = jnp.exp(logits * scale)
    dispatch = (powers / jnp.sum(powers, axis=1, keepdims=True)).astype(jnp.bfloat16)
    slot_in = dot(dispatch, x)

    def message(values, first):
        return jnp.concatenate(
            [
                values[first : first + own, k * part : (k + 1) * part]
                for k in range(fold)
            ],
            axis=0,
        ).astype(jnp.bfloat16)

    for e in range(owners):
        send_in[e] = message(slot_in, e * own)
    pl.semaphore_wait(barrier, peers - 1)

    def send_slots(s):
        _, e, device = peer(s)
        pltpu.make_async_remote_copy(
            src_ref=send_in.at[e],
            dst_ref=recv_in.at[me],
            send_sem=send_sem.at[0],
            recv_sem=recv_sem.at[0],
            device_id=device,
            device_id_type=MESH,
        ).start()

    each(peers, send_slots)
    recv_in[me] = send_in[me_e]

    combine = (powers / jnp.sum(powers, axis=0, keepdims=True)).astype(jnp.bfloat16)
    col = lax.broadcasted_iota(jnp.int32, (columns, peers * ROWS), 0)
    row = lax.broadcasted_iota(jnp.int32, (columns, peers * ROWS), 1)
    col_hit = col == (row // (ROWS * shares)) * own + row % own
    for k in range(fold):
        hit = jnp.logical_and(col_hit, (row // own) % fold == k)
        spread_v[k] = dot(combine, one_hot(hit), ((0,), (0,))).astype(jnp.bfloat16)

    group = min(peers, 16)
    block = group * ROWS

    def by_expert(axis):
        to = lax.broadcasted_iota(jnp.int32, (block, block), axis)
        at = lax.broadcasted_iota(jnp.int32, (block, block), 1 - axis)
        slot = to % SLOTS
        image = (to // SLOTS) % group
        rest = to // (SLOTS * group)
        return one_hot(at == image * ROWS + rest * SLOTS + slot)

    sort = by_expert(0)
    unsort = by_expert(1)

    def all_but_one(buffer, sem):
        view = buffer.at[pl.ds(0, peers - 1)]
        return pltpu.make_async_copy(view, view, sem)

    all_but_one(recv_in, recv_sem.at[0]).wait()

    groups = peers // group
    span = group * SLOTS
    sorted_rows = [
        dot(sort, recv_in[g * group : (g + 1) * group].reshape(block, part)).astype(jnp.bfloat16)
        for g in range(groups)
    ]
    partial = []
    for e in range(experts):
        weights[2 * e].wait()
        hidden = None
        for k in range(fold):
            start = (k * experts + e) * span
            rows = jnp.concatenate([r[start : start + span] for r in sorted_rows], axis=0)
            term = dot(rows, w_in_v[e, k * part : (k + 1) * part, :])
            hidden = term if hidden is None else hidden + term
        hidden = jax.nn.gelu(hidden, approximate=True).astype(jnp.bfloat16)
        weights[2 * e + 1].wait()
        partial.append(dot(hidden, w_out_v[e]).astype(jnp.bfloat16))
    for g in range(groups):
        rows = jnp.concatenate(
            [
                partial[e][g * span : (g + 1) * span, k * part : (k + 1) * part]
                for k in range(fold)
                for e in range(experts)
            ],
            axis=0,
        )
        send_out[g * group : (g + 1) * group] = (
            dot(unsort, rows).astype(jnp.bfloat16).reshape(group, ROWS, part)
        )

    def send_results(s):
        p, _, device = peer(s)
        pltpu.make_async_remote_copy(
            src_ref=send_out.at[p],
            dst_ref=recv_out.at[me],
            send_sem=send_sem.at[1],
            recv_sem=recv_sem.at[1],
            device_id=device,
            device_id_type=MESH,
        ).start()

    each(peers, send_results)
    recv_out[me] = send_out[me]
    all_but_one(recv_in, send_sem.at[0]).wait()
    all_but_one(recv_out, recv_sem.at[1]).wait()
    arrived = recv_out[...].reshape(peers * ROWS, part)
    for k in range(fold):
        out[0, :, k * part : (k + 1) * part] = dot(spread_v[k], arrived).astype(out.dtype)
    all_but_one(send_out, send_sem.at[1]).wait()


def body(images_in, slot_keys, w_in, w_out):
    owners = lax.axis_size("expert")
    shares = lax.axis_size("hid")
    peers = owners * shares
    _, tokens, width = images_in.shape
    own = w_in.shape[0] * SLOTS
    fold = ROWS // own
    part = width // fold
    hbm = pl.BlockSpec(memory_space=pltpu.HBM)
    bf16 = jnp.bfloat16
    return pl.pallas_call(
        functools.partial(kernel, owners, shares),
        out_shape=jax.ShapeDtypeStruct(images_in.shape, bf16),
        in_specs=[hbm] * 4,
        out_specs=pl.BlockSpec(memory_space=pltpu.VMEM),
        scratch_shapes=[
            pltpu.VMEM((tokens, width), bf16),
            pltpu.VMEM(slot_keys.shape[::-1], bf16),
            pltpu.VMEM(w_in.shape, bf16),
            pltpu.VMEM(w_out.shape, bf16),
            pltpu.VMEM((owners, ROWS, part), bf16),
            pltpu.VMEM((peers, ROWS, part), bf16),
            pltpu.VMEM((peers, ROWS, part), bf16),
            pltpu.VMEM((peers, ROWS, part), bf16),
            pltpu.VMEM((fold, tokens, peers * ROWS), bf16),
            pltpu.SemaphoreType.DMA((2 + 2 * w_in.shape[0],)),
            pltpu.SemaphoreType.DMA((2,)),
            pltpu.SemaphoreType.DMA((2,)),
        ],
        compiler_params=pltpu.CompilerParams(
            collective_id=0, has_side_effects=True, vmem_limit_bytes=60 * 1024 * 1024
        ),
    )(images_in, slot_keys.T, w_in, w_out)


def solution(mesh):
    return jax.shard_map(
        body,
        mesh=mesh,
        in_specs=(
            P(("dp", "expert", "hid"), None, None),
            P(),
            P("expert", None, "hid"),
            P("expert", "hid", None),
        ),
        out_specs=P(("dp", "expert", "hid"), None, None),
        check_vma=False,
    )
```

time: 90.2 us -> 21.5 us (0.24)
  waiting for transfers between devices: 34.3 us -> 0 us
  blocking collectives: 28.1 us -> 0 us
  Pallas kernels: 0 us -> 19.5 us
  between operations: 13.4 us -> 0.01 us
  matrix products: 8.95 us -> 0 us
  other arithmetic: 2.12 us -> 0 us
  local copies, waits for them, and re-layouts: 2.83 us -> 1.87 us
    unnamed x2 -> x0, waiting for transfers between devices: 34.3 us -> none
    pallas_call x0 -> x1, Pallas kernels: none -> 19.5 us  [body(): pl.pallas_call(functools.partial(kernel, owners, shares), out_shape=jax.S...]
    all_to_all x2 -> x0, blocking collectives: 14.4 us -> none  [the longest x1 7.95 us: body(): lax.all_to_all(grouped, 'expert', split_axis=1, concat_axis=1, tiled=True)]
    all_gather x1 -> x0, blocking collectives: 13.7 us -> none  [body(): arrived = lax.all_gather(arrived, 'hid', axis=0, tiled=True)]
    dot_general x4 -> x0, matrix products: 8.95 us -> none  [the longest x1 5.04 us: body(): jnp.einsum('rbsf,bfd->rbsd', hidden, w_out, preferred_element_type=jnp.fl...]
    reduce_sum x2 -> x0, other arithmetic: 2.11 us -> none  [the longest x1 1.23 us: normal_rows(): jnp.mean(floats * floats, axis=-1, keepdims=True) + 1e-06]
    reduce_scatter x1 -> x0, local copies, waits for them, and re-layouts: 1.33 us -> none  [body(): lax.psum_scatter(partial_value.astype(jnp.bfloat16), 'hid', scatter_dimen...]
    unnamed x3 -> x1, local copies, waits for them, and re-layouts: 0.58 us -> 1.87 us
  transfers between devices with their start and end apart: 1 -> 0, of which waited for: 1 -> 0; matrix products, arithmetic and copies ran while one was open for 1% -> 0% of each run, Pallas kernels for 0% -> 0%
where the time goes in v1:
time: 21.5 us; the launch traced here: 21.4 us
  Pallas kernels  19.5 us (91%)
  local copies, waits for them, and re-layouts  1.87 us (9%)
    pallas_call x1, Pallas kernels, body(): pl.pallas_call(functools.partial(kernel, owners, shares), out_shape=jax.S...  19.5 us
    unnamed x1, local copies, waits for them, and re-layouts  1.87 us

profile of v1, /device:TPU:0, one launch (start us, length us, event | category | flops | bytes accessed | tf_op | source)
XLA Modules:
  0.0 21.4 jit_solution(3060904816699741527)
XLA Ops:
  0.0 19.5 %shard_map.46 = bf16[1,256,1024]{2,1,0:T(8,128)(2,1)} custom-call(bf16[1,256,1024]{2,1,0:T(8,128)(2,1)} %x_hbm.1, bf16[16,1024]{1,0:T(8,128)(2,1)} %bitcast.1, bf16[2,1024,1024]{2,1,0:T(8,128)(2,1)} %w_in_hbm.1, bf16[2,1024,1024]{2,1,0:T(8,128)(2,1)} %w_out_hbm.1), custom_call_target="tpu_custom_call" | custom-call | tf_op jit(solution)/shard_map/pallas_call | solution.py:233
  19.5 1.9 %copy.6 = bf16[1,256,1024]{2,1,0:T(8,128)(2,1)} copy(bf16[1,256,1024]{2,1,0:T(8,128)(2,1)} %shard_map.46) | data formatting | bytes 1048576

commit v2 on v1

--- a/solution.py
+++ b/solution.py
@@ -64,24 +64,38 @@
     part = width // fold
     me_e = lax.axis_index("expert")
     me_h = lax.axis_index("hid")
-    me = me_e * shares + me_h
+    me = me_h * owners + me_e
 
     x_copy = pltpu.make_async_copy(x_hbm.at[0], x_v, local_sem.at[0])
     keys_copy = pltpu.make_async_copy(keys_hbm, keys_v, local_sem.at[1])
     x_copy.start()
     keys_copy.start()
 
+    def at(p):
+        return {"expert": lax.rem(p, owners), "hid": lax.div(p, owners)}
+
     def peer(s):
         p = lax.rem(me + s, peers)
-        e = lax.div(p, shares)
-        return p, e, {"expert": e, "hid": lax.rem(p, shares)}
+        return p, at(p)
 
     barrier = pltpu.get_barrier_semaphore()
 
     def greet(s):
-        pl.semaphore_signal(barrier, inc=1, device_id=peer(s)[2], device_id_type=MESH)
+        pl.semaphore_signal(barrier, inc=1, device_id=peer(s)[1], device_id_type=MESH)
 
     each(peers, greet)
+
+    def by_expert(group, axis):
+        to = lax.broadcasted_iota(jnp.int32, (group * ROWS, group * ROWS), axis)
+        from_ = lax.broadcasted_iota(jnp.int32, (group * ROWS, group * ROWS), 1 - axis)
+        slot = to % SLOTS
+        image = (to // SLOTS) % group
+        rest = to // (SLOTS * group)
+        return one_hot(from_ == image * ROWS + rest * SLOTS + slot)
+
+    group = max(g for g in range(1, 17) if peers % g == 0)
+    sort = by_expert(group, 0)
+    unsort = by_expert(group, 1)
 
     keys_copy.wait()
     keys = keys_v[...].astype(jnp.float32)
@@ -126,98 +140,98 @@
         send_in[e] = message(slot_in, e * own)
     pl.semaphore_wait(barrier, peers - 1)
 
-    def send_slots(s):
-        _, e, device = peer(s)
-        pltpu.make_async_remote_copy(
-            src_ref=send_in.at[e],
-            dst_ref=recv_in.at[me],
-            send_sem=send_sem.at[0],
-            recv_sem=recv_sem.at[0],
-            device_id=device,
-            device_id_type=MESH,
-        ).start()
-
+    def far_first(j):
+        h = lax.div(j, owners)
+        h = jnp.where(2 * me_h < shares, shares - 1 - h, h)
+        return h * owners + lax.rem(me_e + 1 + j, owners)
+
+    def send_slots(j):
+        p = far_first(j)
+
+        @pl.when(p != me)
+        def _():
+            pltpu.make_async_remote_copy(
+                src_ref=send_in.at[lax.rem(p, owners)],
+                dst_ref=recv_in.at[me],
+                send_sem=send_sem.at[0],
+                recv_sem=recv_sem.at[0],
+                device_id=at(p),
+                device_id_type=MESH,
+            ).start()
+
+    send_slots(0)
     each(peers, send_slots)
-    recv_in[me] = send_in[me_e]
-
-    combine = (powers / jnp.sum(powers, axis=0, keepdims=True)).astype(jnp.bfloat16)
-    col = lax.broadcasted_iota(jnp.int32, (columns, peers * ROWS), 0)
-    row = lax.broadcasted_iota(jnp.int32, (columns, peers * ROWS), 1)
-    col_hit = col == (row // (ROWS * shares)) * own + row % own
-    for k in range(fold):
-        hit = jnp.logical_and(col_hit, (row // own) % fold == k)
-        spread_v[k] = dot(combine, one_hot(hit), ((0,), (0,))).astype(jnp.bfloat16)
-
-    group = min(peers, 16)
+    pltpu.make_async_copy(send_in.at[me_e], recv_in.at[me], recv_sem.at[0]).start()
+
+    def arrival(buffer, sem, count):
+        view = buffer.at[pl.ds(0, count)]
+        return pltpu.make_async_copy(view, view, sem)
+
     block = group * ROWS
-
-    def by_expert(axis):
-        to = lax.broadcasted_iota(jnp.int32, (block, block), axis)
-        at = lax.broadcasted_iota(jnp.int32, (block, block), 1 - axis)
-        slot = to % SLOTS
-        image = (to // SLOTS) % group
-        rest = to // (SLOTS * group)
-        return one_hot(at == image * ROWS + rest * SLOTS + slot)
-
-    sort = by_expert(0)
-    unsort = by_expert(1)
-
-    def all_but_one(buffer, sem):
-        view = buffer.at[pl.ds(0, peers - 1)]
-        return pltpu.make_async_copy(view, view, sem)
-
-    all_but_one(recv_in, recv_sem.at[0]).wait()
-
-    groups = peers // group
     span = group * SLOTS
+    arrival(recv_in, recv_sem.at[0], peers).wait()
+    starts = range(0, peers, group)
     sorted_rows = [
-        dot(sort, recv_in[g * group : (g + 1) * group].reshape(block, part)).astype(jnp.bfloat16)
-        for g in range(groups)
+        dot(sort, recv_in[g : g + group].reshape(block, part)).astype(jnp.bfloat16)
+        for g in starts
     ]
     partial = []
     for e in range(experts):
         weights[2 * e].wait()
         hidden = None
         for k in range(fold):
-            start = (k * experts + e) * span
-            rows = jnp.concatenate([r[start : start + span] for r in sorted_rows], axis=0)
+            at_row = (k * experts + e) * span
+            rows = jnp.concatenate([r[at_row : at_row + span] for r in sorted_rows], axis=0)
             term = dot(rows, w_in_v[e, k * part : (k + 1) * part, :])
             hidden = term if hidden is None else hidden + term
         hidden = jax.nn.gelu(hidden, approximate=True).astype(jnp.bfloat16)
         weights[2 * e + 1].wait()
         partial.append(dot(hidden, w_out_v[e]).astype(jnp.bfloat16))
-    for g in range(groups):
+    for i, g in enumerate(starts):
         rows = jnp.concatenate(
             [
-                partial[e][g * span : (g + 1) * span, k * part : (k + 1) * part]
+                partial[e][i * span : (i + 1) * span, k * part : (k + 1) * part]
                 for k in range(fold)
                 for e in range(experts)
             ],
             axis=0,
         )
-        send_out[g * group : (g + 1) * group] = (
+        send_out[g : g + group] = (
             dot(unsort, rows).astype(jnp.bfloat16).reshape(group, ROWS, part)
         )
 
-    def send_results(s):
-        p, _, device = peer(s)
-        pltpu.make_async_remote_copy(
-            src_ref=send_out.at[p],
-            dst_ref=recv_out.at[me],
-            send_sem=send_sem.at[1],
-            recv_sem=recv_sem.at[1],
-            device_id=device,
-            device_id_type=MESH,
-        ).start()
-
-    each(peers, send_results)
-    recv_out[me] = send_out[me]
-    all_but_one(recv_in, send_sem.at[0]).wait()
-    all_but_one(recv_out, recv_sem.at[1]).wait()
+    def send_result(j):
+        p = far_first(j)
+
+        @pl.when(p != me)
+        def _():
+            pltpu.make_async_remote_copy(
+                src_ref=send_out.at[p],
+                dst_ref=recv_out.at[me],
+                send_sem=send_sem.at[1],
+                recv_sem=recv_sem.at[1],
+                device_id=at(p),
+                device_id_type=MESH,
+            ).start()
+
+    send_result(0)
+    each(peers, send_result)
+
+    combine = (powers / jnp.sum(powers, axis=0, keepdims=True)).astype(jnp.bfloat16)
+    col = lax.broadcasted_iota(jnp.int32, (columns, peers * ROWS), 0)
+    row = lax.broadcasted_iota(jnp.int32, (columns, peers * ROWS), 1)
+    col_hit = col == ((row // ROWS) % owners) * own + row % own
+    for k in range(fold):
+        hit = jnp.logical_and(col_hit, (row // own) % fold == k)
+        spread_v[k] = dot(combine, one_hot(hit), ((0,), (0,))).astype(jnp.bfloat16)
+
+    pltpu.make_async_copy(send_out.at[me], recv_out.at[me], recv_sem.at[1]).start()
+    arrival(recv_out, recv_sem.at[1], peers).wait()
     arrived = recv_out[...].reshape(peers * ROWS, part)
     for k in range(fold):
         out[0, :, k * part : (k + 1) * part] = dot(spread_v[k], arrived).astype(out.dtype)
-    all_but_one(send_out, send_sem.at[1]).wait()
+    arrival(recv_in, send_sem.at[0], peers - 1).wait()
+    arrival(send_out, send_sem.at[1], peers - 1).wait()
 
 
 def body(images_in, slot_keys, w_in, w_out):
@@ -232,7 +246,7 @@
     bf16 = jnp.bfloat16
     return pl.pallas_call(
         functools.partial(kernel, owners, shares),
-        out_shape=jax.ShapeDtypeStruct(images_in.shape, bf16),
+        out_shape=pltpu.VMEM(images_in.shape, bf16),
         in_specs=[hbm] * 4,
         out_specs=pl.BlockSpec(memory_space=pltpu.VMEM),
         scratch_shapes=[

time: 21.5 us -> 19 us (0.88)
  Pallas kernels: 19.5 us -> 18.1 us
  local copies, waits for them, and re-layouts: 1.87 us -> 0.8 us
    pallas_call x1, Pallas kernels: 19.5 us -> 18.1 us  [body(): pl.pallas_call(functools.partial(kernel, owners, shares), out_shape=pltpu...]
    unnamed x1, local copies, waits for them, and re-layouts: 1.87 us -> 0.8 us
where the time goes in v2:
time: 19 us; the launch traced here: 18.9 us
  Pallas kernels  18.1 us (95%)
  local copies, waits for them, and re-layouts  0.8 us (4%)
    pallas_call x1, Pallas kernels, body(): pl.pallas_call(functools.partial(kernel, owners, shares), out_shape=pltpu...  18.1 us
    unnamed x1, local copies, waits for them, and re-layouts  0.8 us

profile of v2, /device:TPU:0, one launch (start us, length us, event | category | flops | bytes accessed | tf_op | source)
XLA Modules:
  0.0 18.9 jit_solution(7066640292212976236)
XLA Ops:
  0.0 18.1 %shard_map.46 = bf16[1,256,1024]{2,1,0:T(8,128)(2,1)S(1)} custom-call(bf16[1,256,1024]{2,1,0:T(8,128)(2,1)} %x_hbm.1, bf16[16,1024]{1,0:T(8,128)(2,1)} %bitcast.1, bf16[2,1024,1024]{2,1,0:T(8,128)(2,1)} %w_in_hbm.1, bf16[2,1024,1024]{2,1,0:T(8,128)(2,1)} %w_out_hbm.1), custom_call_target="tpu_custom_call" | custom-call | tf_op jit(solution)/shard_map/pallas_call | solution.py:247
  18.1 0.8 %copy.6 = bf16[1,256,1024]{2,1,0:T(8,128)(2,1)} copy(bf16[1,256,1024]{2,1,0:T(8,128)(2,1)S(1)} %shard_map.46) | data formatting | bytes 1048576

commit v3 on v2

--- a/solution.py
+++ b/solution.py
@@ -85,24 +85,6 @@
 
     each(peers, greet)
 
-    def by_expert(group, axis):
-        to = lax.broadcasted_iota(jnp.int32, (group * ROWS, group * ROWS), axis)
-        from_ = lax.broadcasted_iota(jnp.int32, (group * ROWS, group * ROWS), 1 - axis)
-        slot = to % SLOTS
-        image = (to // SLOTS) % group
-        rest = to // (SLOTS * group)
-        return one_hot(from_ == image * ROWS + rest * SLOTS + slot)
-
-    group = max(g for g in range(1, 17) if peers % g == 0)
-    sort = by_expert(group, 0)
-    unsort = by_expert(group, 1)
-
-    keys_copy.wait()
-    keys = keys_v[...].astype(jnp.float32)
-    unit = (keys * lax.rsqrt(jnp.sum(keys * keys, axis=1, keepdims=True) + 1e-06)).astype(
-        jnp.bfloat16
-    )
-    x_copy.wait()
     weights = []
     for e in range(experts):
         for k, (hbm, vmem) in enumerate(((w_in_hbm, w_in_v), (w_out_hbm, w_out_v))):
@@ -112,6 +94,24 @@
     for copy in weights[0::2] + weights[1::2]:
         copy.start()
 
+    def by_expert(group, axis):
+        to = lax.broadcasted_iota(jnp.int32, (group * ROWS, group * ROWS), axis)
+        from_ = lax.broadcasted_iota(jnp.int32, (group * ROWS, group * ROWS), 1 - axis)
+        slot = to % SLOTS
+        image = (to // SLOTS) % group
+        rest = to // (SLOTS * group)
+        return one_hot(from_ == image * ROWS + rest * SLOTS + slot)
+
+    group = max(g for g in range(1, 17) if peers % g == 0)
+    sort = by_expert(group, 0)
+    unsort = by_expert(group, 1)
+
+    keys_copy.wait()
+    keys = keys_v[...].astype(jnp.float32)
+    unit = (keys * lax.rsqrt(jnp.sum(keys * keys, axis=1, keepdims=True) + 1e-06)).astype(
+        jnp.bfloat16
+    )
+    x_copy.wait()
     x = x_v[...]
     logits = dot(unit, x, ((1,), (1,)))
     squares = None
@@ -169,6 +169,8 @@
 
     block = group * ROWS
     span = group * SLOTS
+    for copy in weights:
+        copy.wait()
     arrival(recv_in, recv_sem.at[0], peers).wait()
     starts = range(0, peers, group)
     sorted_rows = [
@@ -176,8 +178,8 @@
         for g in starts
     ]
     partial = []
+    hiddens = []
     for e in range(experts):
-        weights[2 * e].wait()
         hidden = None
         for k in range(fold):
             at_row = (k * experts + e) * span
@@ -185,8 +187,9 @@
             term = dot(rows, w_in_v[e, k * part : (k + 1) * part, :])
             hidden = term if hidden is None else hidden + term
         hidden = jax.nn.gelu(hidden, approximate=True).astype(jnp.bfloat16)
-        weights[2 * e + 1].wait()
-        partial.append(dot(hidden, w_out_v[e]).astype(jnp.bfloat16))
+        hiddens.append(hidden)
+    for e in range(experts):
+        partial.append(dot(hiddens[e], w_out_v[e]).astype(jnp.bfloat16))
     for i, g in enumerate(starts):
         rows = jnp.concatenate(
             [
@@ -200,21 +203,17 @@
             dot(unsort, rows).astype(jnp.bfloat16).reshape(group, ROWS, part)
         )
 
-    def send_result(j):
-        p = far_first(j)
-
-        @pl.when(p != me)
-        def _():
-            pltpu.make_async_remote_copy(
-                src_ref=send_out.at[p],
-                dst_ref=recv_out.at[me],
-                send_sem=send_sem.at[1],
-                recv_sem=recv_sem.at[1],
-                device_id=at(p),
-                device_id_type=MESH,
-            ).start()
-
-    send_result(0)
+    def send_result(s):
+        p = lax.rem(me + s, peers)
+        pltpu.make_async_remote_copy(
+            src_ref=send_out.at[p],
+            dst_ref=recv_out.at[me],
+            send_sem=send_sem.at[1],
+            recv_sem=recv_sem.at[1],
+            device_id=at(p),
+            device_id_type=MESH,
+        ).start()
+
     each(peers, send_result)
 
     combine = (powers / jnp.sum(powers, axis=0, keepdims=True)).astype(jnp.bfloat16)

time: 19 us -> 18 us (0.947)
  Pallas kernels: 18.1 us -> 17.1 us
    pallas_call x1, Pallas kernels: 18.1 us -> 17.1 us  [body(): pl.pallas_call(functools.partial(kernel, owners, shares), out_shape=pltpu...]
where the time goes in v3:
time: 18 us; the launch traced here: 17.9 us
  Pallas kernels  17.1 us (95%)
  local copies, waits for them, and re-layouts  0.8 us (4%)
    pallas_call x1, Pallas kernels, body(): pl.pallas_call(functools.partial(kernel, owners, shares), out_shape=pltpu...  17.1 us
    unnamed x1, local copies, waits for them, and re-layouts  0.8 us

profile of v3, /device:TPU:0, one launch (start us, length us, event | category | flops | bytes accessed | tf_op | source)
XLA Modules:
  0.0 17.9 jit_solution(11762027781656820804)
XLA Ops:
  0.0 17.1 %shard_map.46 = bf16[1,256,1024]{2,1,0:T(8,128)(2,1)S(1)} custom-call(bf16[1,256,1024]{2,1,0:T(8,128)(2,1)} %x_hbm.1, bf16[16,1024]{1,0:T(8,128)(2,1)} %bitcast.1, bf16[2,1024,1024]{2,1,0:T(8,128)(2,1)} %w_in_hbm.1, bf16[2,1024,1024]{2,1,0:T(8,128)(2,1)} %w_out_hbm.1), custom_call_target="tpu_custom_call" | custom-call | tf_op jit(solution)/shard_map/pallas_call | solution.py:246
  17.1 0.8 %copy.6 = bf16[1,256,1024]{2,1,0:T(8,128)(2,1)} copy(bf16[1,256,1024]{2,1,0:T(8,128)(2,1)S(1)} %shard_map.46) | data formatting | bytes 1048576
